TPU v7x, 256 devices: a whole 4x4x8 slice. The times are simulated.
256 devices in a mesh: vocab: 32 (over x, z), hid: 8 (over y, core).
Axes of the slice: x: 4, y: 4, z: 8, core: 2. Of those that a mesh axis runs over, the one named last changes fastest.
Arguments:
- student_hidden: bfloat16 [1024, 8192], P(None, 'hid'), as said below
- head_weight: bfloat16 [8192, 65536], P('hid', 'vocab'), as said below
- teacher_logits: bfloat16 [1024, 65536], P(('vocab', 'hid')), as said below
Outputs:
- loss_value: float32 [], replicated
- grad_hidden: bfloat16 [1024, 8192], P('vocab', 'hid')
- grad_weight: bfloat16 [8192, 65536], P('hid', 'vocab')
Inputs may be any that keep to these rules, and one draw needn't show every extreme that they name: `student_hidden`: hidden states of order one to some tens. `head_weight`: weights of order one over the square root of 8192. `teacher_logits`: logits of order one to some hundreds.
All inputs are finite; a program needn't handle non-finite values.
Results may differ from a plain program's by a relative error of at most 0.02055.
Values may be sent and summed in bfloat16 or wider, within the bound.
No kernel may reach another device: no remote copies, remote signals or barrier semaphores. Data moves between devices by JAX's collectives and lax.ppermute only.
A program may use at most 128 MiB of HBM per device.

v0:
```python
import jax
import jax.numpy as jnp
from jax import lax
from jax.sharding import PartitionSpec as P


def row_terms(logits, teacher):
    top_student, top_teacher = lax.pmax(
        (jnp.max(logits, axis=1), jnp.max(teacher, axis=1)), "vocab"
    )
    total_student, total_teacher = lax.psum(
        (
            jnp.sum(jnp.exp(logits - top_student[:, None]), axis=1),
            jnp.sum(jnp.exp(teacher - top_teacher[:, None]), axis=1),
        ),
        "vocab",
    )
    student_log = logits - (top_student + jnp.log(total_student))[:, None]
    teacher_log = teacher - (top_teacher + jnp.log(total_teacher))[:, None]
    probs = jnp.exp(student_log)
    kl_row = lax.psum(jnp.sum(probs * (student_log - teacher_log), axis=1), "vocab")
    return (kl_row, student_log, teacher_log, probs)


def shards(student_hidden, head_weight, teacher_logits):
    n_vocab = lax.axis_size("vocab")
    tokens = student_hidden.shape[0]
    vocab_width = head_weight.shape[1]
    per_dev = teacher_logits.shape[0]
    partial_value = jnp.dot(student_hidden, head_weight, preferred_element_type=jnp.float32)
    teacher_tiles = lax.all_to_all(teacher_logits, "vocab", split_axis=1, concat_axis=0, tiled=True)
    logits = lax.psum(partial_value, "hid")
    stacked = lax.all_gather(
        teacher_tiles.reshape(n_vocab, 1, per_dev, vocab_width), "hid", axis=1, tiled=True
    )
    teacher = stacked.reshape(tokens, vocab_width).astype(jnp.float32)
    kl_row, student_log, teacher_log, probs = row_terms(logits, teacher)
    grad_logits = (probs * (student_log - teacher_log - kl_row[:, None]) / tokens).astype(
        jnp.bfloat16
    )
    loss_value = jnp.sum(kl_row) / tokens
    grad_hidden = lax.psum_scatter(
        lax.dot_general(
            grad_logits, head_weight, (((1,), (1,)), ((), ())), preferred_element_type=jnp.float32
        ).astype(jnp.bfloat16),
        "vocab",
        scatter_dimension=0,
        tiled=True,
    )
    grad_weight = lax.dot_general(
        student_hidden, grad_logits, (((0,), (0,)), ((), ())), preferred_element_type=jnp.float32
    ).astype(jnp.bfloat16)
    return (loss_value, grad_hidden, grad_weight)


def solution(mesh):
    in_specs = (P(None, "hid"), P("hid", "vocab"), P(("vocab", "hid"), None))
    out_specs = (P(), P("vocab", "hid"), P("hid", "vocab"))
    return jax.shard_map(shards, mesh=mesh, in_specs=in_specs, out_specs=out_specs, check_vma=False)
```

profile of v0, /device:TPU:24, one launch (start us, length us, event | category | flops | bytes accessed | tf_op | source)
XLA Modules:
  0.0 647.9 jit_solution(4243256901475709458)
XLA Ops:
  7.2 1.5 copy-done
  8.8 8.8 %fusion.2 = f32[1024,2048]{1,0:T(8,128)} fusion(bf16[1024,1024]{1,0:T(8,128)(2,1)S(1)} %copy-done, bf16[1024,2048]{1,0:T(8,128)(2,1)} %param.4), kind=kOutput, calls=%fused_computation.11 | convolution fusion | flops 4294967296 | bytes 14680064 | tf_op jit(solution)/shard_map/dot_general | solution.py:30
  17.6 0.0 all-gather.3.cloned.1.call-start
  17.7 1.0 copy-done.3
  18.6 28.0 %all_to_all.16 = bf16[4,32,2048]{2,0,1:T(4,128)(2,1)S(1)} all-to-all(bf16[4,32,2048]{2,0,1:T(4,128)(2,1)S(1)} %bitcast.21), channel_id=1, replica_groups=mesh['vocab'=32,'hid'=8] {'vocab'}, dimensions={1} | all-to-all | bytes 1048576 | tf_op jit(solution)/shard_map/all_to_all | solution.py:31
  46.6 1.1 copy.18
  47.7 0.0 reduce-scatter.2.cloned.1.call-start
  47.8 79.9 %all-reduce.4.cloned.1.call-done = f32[1024,2048]{1,0:T(8,128)} async-done(((f32[1024,2048]{1,0:T(8,128)}), f32[1024,2048]{1,0:T(8,128)}) %all-reduce.4.cloned.1.call-update) | async-done | bytes 8388624 | tf_op jit(solution)/shard_map/psum | solution.py:32
  127.7 3.8 reduce_max.25
  131.5 33.1 %all-gather.3.cloned.1.call-done = bf16[32,32,2048]{2,0,1:T(8,128)(2,1)} async-done(((bf16[32,4,2048]{2,0,1:T(8,128)(2,1)}), bf16[32,32,2048]{2,0,1:T(8,128)(2,1)}) %all-gather.3.cloned.1.call-update) | async-done | bytes 4194320 | tf_op jit(solution)/shard_map/all_gather | solution.py:33
  164.6 8.4 %fusion.1 = (f32[32,32,2048]{2,0,1:T(8,128)}, bf16[32,32]{0,1:T(8,128)(2,1)S(1)}) fusion(bf16[32,32,2048]{2,0,1:T(8,128)(2,1)} %all-gather.3.cloned.1.call-done), kind=kLoop, calls=%fused_computation.10 | loop fusion | flops 4193280 | bytes 12584960 | tf_op jit(solution)/shard_map/convert_element_type | solution.py:36
  173.0 0.1 copy.20
  173.1 0.1 reshape.32
  173.2 76.1 %all-reduce.1 = (f32[1024]{0:T(1024)S(1)}, f32[1024]{0:T(1024)S(1)}) all-reduce(f32[1024]{0:T(1024)S(1)} %reshape.32, f32[1024]{0:T(1024)S(1)} %reduce_max.25), channel_id=1, replica_groups=mesh['vocab'=32,'hid'=8] {'vocab'}, use_global_device_ids=true, to_apply=%region_6.0 | all-reduce | flops 2048 | bytes 16384 | tf_op jit(solution)/shard_map/pmax | solution.py:8
  249.3 0.1 sub.51
  249.4 0.1 copy.21
  249.5 4.7 exponential_reduce_fusion
  254.2 0.1 copy.22
  254.3 0.1 reduce_sum.40
  254.5 4.6 exponential_reduce_fusion.1
  259.1 70.7 %all-reduce = (f32[1024]{0:T(1024)S(1)}, f32[1024]{0:T(1024)S(1)}) all-reduce(f32[1024]{0:T(1024)S(1)} %reduce_sum.40, f32[1024]{0:T(1024)S(1)} %exponential_reduce_fusion.1), channel_id=1, replica_groups=mesh['vocab'=32,'hid'=8] {'vocab'}, use_global_device_ids=true, to_apply=%region_8.0 | all-reduce | flops 2048 | bytes 16384 | tf_op jit(solution)/shard_map/psum | solution.py:11
  329.8 4.6 copy.19
  334.4 3.2 copy-done.1
  337.6 4.8 multiply_reduce_fusion
  342.4 71.8 %psum.31 = f32[1024]{0:T(1024)S(1)} all-reduce(f32[1024]{0:T(1024)S(1)} %multiply_reduce_fusion), channel_id=1, replica_groups=mesh['vocab'=32,'hid'=8] {'vocab'}, use_global_device_ids=true, to_apply=%region_10.0 | all-reduce | flops 1024 | bytes 8192 | tf_op jit(solution)/shard_map/psum | solution.py:21
  414.2 7.4 %multiply_convert_fusion = bf16[1024,2048]{1,0:T(8,128)(2,1)S(1)} fusion(f32[1024,2048]{1,0:T(8,128)} %all-reduce.4.cloned.1.call-done, f32[32,32,2048]{2,1,0:T(8,128)} %copy-done.1, f32[1024]{0:T(1024)S(1)} %psum.31, f32[1024]{0:T(1024)S(1)} %get-tuple-element.24, f32[1024]{0:T(1024)S(1)} %get-tuple-element.25), kind=kLoop, calls=%fused_computation.2 | loop fusion | flops 14680064 | bytes 20983808 | tf_op jit(solution)/shard_map/convert_element_type | solution.py:38
  421.7 2.0 copy-done.2
  423.7 5.8 convolution_convert_fusion
  429.5 8.4 %convert_bitcast_fusion = bf16[1024,2048]{0,1:T(8,128)(2,1)} fusion(bf16[1024,2048]{1,0:T(8,128)(2,1)} %copy-done.2, bf16[1024,1024]{1,0:T(8,128)(2,1)S(1)} %copy-done), kind=kOutput, calls=%fused_computation.6 | convolution fusion | flops 4297064448 | bytes 10485760 | tf_op jit(solution)/shard_map/dot_general | solution.py:50
  437.9 6.4 copy.23
  444.4 0.6 reduce_sum.42
  445.6 194.6 %reduce-scatter.2.cloned.1.call-done = bf16[32,1024]{1,0:T(8,128)(2,1)} async-done(((bf16[1024,1024]{1,0:T(8,128)(2,1)}), bf16[32,1024]{1,0:T(8,128)(2,1)}) %reduce-scatter.2.cloned.1.call-update) | async-done | bytes 65552 | tf_op jit(solution)/shard_map/reduce_scatter | solution.py:42
  (11 shorter events, 0.1 us)
Async XLA Ops:
  7.2 1.6 copy-start
  7.2 120.5 %all-reduce.4.cloned.1.call-start = ((), (), s32[]{:S(2)}) async-start(), calls=%async_computation.2 | async-start | bytes 16777216 | tf_op jit(solution)/shard_map/psum | solution.py:32
  17.6 1.0 copy-start.3
  17.6 147.0 %all-gather.3.cloned.1.call-start = ((), (), s32[]{:S(2)}) async-start(), calls=%async_computation.4 | async-start | bytes 4718592 | tf_op jit(solution)/shard_map/all_gather | solution.py:33
  47.7 592.6 %reduce-scatter.2.cloned.1.call-start = ((), (), s32[]{:S(2)}) async-start(), calls=%async_computation.3 | async-start | bytes 2162688 | tf_op jit(solution)/shard_map/reduce_scatter | solution.py:42
  334.4 3.2 copy-start.1
  414.2 9.5 %copy-start.4 = (bf16[1024,2048]{1,0:T(8,128)(2,1)S(1)}, bf16[1024,2048]{1,0:T(8,128)(2,1)}, u32[]{:S(2)}) copy-start(bf16[1024,2048]{1,0:T(8,128)(2,1)} %param.4) | copy-start | bytes 12582916
  421.6 2.0 copy-start.2
Sparse Core Ops, SparseCore 0:
  17.7 109.9 all-reduce.3
  130.1 34.4 all-gather.2
  429.6 210.5 reduce-scatter.1
where the time goes:
time: 649 us; the launch traced here: 648 us
  waiting for transfers between devices  308 us (47%)
  blocking collectives  247 us (38%)
  other arithmetic  34.3 us (5%)
  matrix products  23.1 us (4%)
  local copies, waits for them, and re-layouts  20.5 us (3%)
  between operations  15.6 us (2%)
    reduce_scatter x1, waiting for transfers between devices, shards(): lax.psum_scatter(lax.dot_general(grad_logits, head_weight, (((1,), (1,)),...  195 us
    psum x1, waiting for transfers between devices, shards(): logits = lax.psum(partial_value, 'hid')  79.9 us
    pmax x1, blocking collectives, row_terms(): lax.pmax((jnp.max(logits, axis=1), jnp.max(teacher, axis=1)), 'vocab')  76.1 us
    psum x1, blocking collectives, row_terms(): lax.psum(jnp.sum(probs * (student_log - teacher_log), axis=1), 'vocab')  71.8 us
    psum x1, blocking collectives, row_terms(): lax.psum((jnp.sum(jnp.exp(logits - top_student[:, None]), axis=1), jnp.su...  70.7 us
    all_gather x1, waiting for transfers between devices, shards(): lax.all_gather(teacher_tiles.reshape(n_vocab, 1, per_dev, vocab_width), '...  33.1 us
    all_to_all x1, blocking collectives, shards(): lax.all_to_all(teacher_logits, 'vocab', split_axis=1, concat_axis=0, tile...  28 us
    unnamed x11, local copies, waits for them, and re-layouts  14.2 us
  transfers between devices with their start and end apart: 3, of which 3 were waited for; matrix products, arithmetic and copies ran while one was open for 3% of the time, Pallas kernels for 0%

commit v1 on v0

v1 whole, which is shorter than its diff:
```python
import jax
import jax.numpy as jnp
from jax import lax
from jax.sharding import PartitionSpec as P

BF16 = jnp.bfloat16
F32 = jnp.float32
NX, NZ, NY = 4, 8, 4


def to_core(a):
    return lax.ppermute(a, "hid", [(i, i ^ 1) for i in range(2 * NY)])


def to_y(a, d):
    return lax.ppermute(a, "hid", [(i, (i + 2 * d) % (2 * NY)) for i in range(2 * NY)])


def to_x(a, d):
    return lax.ppermute(a, "vocab", [(i, (i + NZ * d) % (NX * NZ)) for i in range(NX * NZ)])


def take(a, i):
    return lax.dynamic_index_in_dim(a, i, 0, keepdims=False)


def shards(student_hidden, head_weight, teacher_logits):
    n_vocab = NX * NZ
    tokens, depth = student_hidden.shape
    width = head_weight.shape[1]
    hid = lax.axis_index("hid")
    y, core = hid // 2, hid % 2
    x = lax.axis_index("vocab") // NZ
    rows = tokens // 8
    by_y = student_hidden.reshape(2, 16, NY, 8, depth)
    mine, other = take(by_y, core), take(by_y, 1 - core)

    def rows_of(part, d):
        return lax.dynamic_index_in_dim(part, (y + d) % NY, 1, keepdims=False).reshape(rows, depth)

    order = (2, 1, 3, 0)
    hid_other = jnp.concatenate([rows_of(other, d) for d in order])
    hid_mine = jnp.concatenate([rows_of(mine, d) for d in order])

    def dot(a):
        return jnp.dot(a, head_weight, preferred_element_type=F32)

    got_a = to_core(dot(hid_other[:rows]))
    got_b = to_core(dot(hid_other[rows:]))
    part = dot(hid_mine)
    u2 = part[:rows] + got_a
    half = rows // 2
    r1 = to_y(u2[:half], 1)
    r2 = to_y(u2[half:], -1)
    u1 = part[rows : 2 * rows] + got_b[:rows]
    u3 = part[2 * rows : 3 * rows] + got_b[rows : 2 * rows]
    u0 = part[3 * rows :] + got_b[2 * rows :]
    r3 = to_y(u1[half:], 1)
    r4 = to_y(u3[:half], -1)
    tiles = lax.all_to_all(teacher_logits, "vocab", split_axis=1, concat_axis=0, tiled=True)
    tiles = tiles.reshape(2, 16, 4, width)
    theirs = to_core(take(tiles, 1 - core))
    own = take(tiles, core)
    both = jnp.stack([own, theirs])
    teacher = jnp.stack([take(both, core), take(both, 1 - core)], axis=1).reshape(rows, width).astype(F32)
    r5 = to_y(u1[:half] + r1, 1)
    r6 = to_y(u3[half:] + r2, -1)
    logits = u0 + jnp.concatenate([r4 + r5, r3 + r6])

    m = jnp.max(logits, axis=1)
    mt = jnp.max(teacher, axis=1)
    ls = logits - m[:, None]
    lt = teacher - mt[:, None]
    e = jnp.exp(ls)
    s = jnp.sum(e, axis=1)
    st = jnp.sum(jnp.exp(lt), axis=1)
    cross = jnp.sum(e * (ls - lt), axis=1)
    terms = jnp.stack([m, s, mt, st, cross, m, m, m])
    terms = jnp.broadcast_to(terms[None], (n_vocab, 8, rows))
    terms = lax.all_to_all(terms, "vocab", split_axis=0, concat_axis=0, tiled=True)
    gm, gs, gmt, gst, gc = (terms[:, i] for i in range(5))
    top, top_t = jnp.max(gm, axis=0), jnp.max(gmt, axis=0)
    w = jnp.exp(gm - top)
    total = jnp.sum(gs * w, axis=0)
    total_t = jnp.sum(gst * jnp.exp(gmt - top_t), axis=0)
    log_total, log_total_t = jnp.log(total), jnp.log(total_t)
    mean_ratio = jnp.sum(w * (gc + gs * ((gm - top) - (gmt - top_t))), axis=0) / total
    kl_row = mean_ratio - log_total + log_total_t
    lse = top + log_total
    lse_t = top_t + log_total_t

    student_log = logits - lse[:, None]
    teacher_log = teacher - lse_t[:, None]
    probs = jnp.exp(student_log)
    grad = (probs * (student_log - teacher_log - kl_row[:, None]) / tokens).astype(BF16)

    g1, g2 = grad[:half], grad[half:]
    a1, a2 = to_y(g1, 1), to_y(g2, -1)
    own_b = to_core(grad)
    a3, a4 = to_y(g2, 1), to_y(g1, -1)
    a5, a6 = to_y(a1, 1), to_y(a2, -1)
    near = jnp.concatenate([a4, a2, a1, a3])
    far = jnp.concatenate([a5, a6])
    near_b = to_core(near)
    far_b = to_core(far)
    grads = jnp.concatenate([far, near, grad, far_b, near_b, own_b])
    hiddens = jnp.concatenate([hid_mine, hid_other])
    part_hidden = lax.dot_general(
        grads, head_weight, (((1,), (1,)), ((), ())), preferred_element_type=F32
    ).astype(BF16)
    part_hidden = part_hidden.reshape(2, NY, 2, NZ, 8, depth)

    def for_x(d):
        to = (x + d) % NX
        which = jnp.where(to // 2 == core, 0, 1)
        piece = lax.dynamic_slice(
            part_hidden, (which, 0, to % 2, 0, 0, 0), (1, NY, 1, NZ, 8, depth)
        )
        return piece.reshape(NY, NZ, 8, depth)

    got = [to_x(for_x(d), d) for d in (2, 1, 3)]
    summed = for_x(0).astype(F32)
    for g in got:
        summed = summed + g.astype(F32)
    summed = summed.astype(BF16).transpose(1, 0, 2, 3).reshape(NZ * NY * 8, depth)
    z_groups = [[i * NZ + j for j in range(NZ)] for i in range(NX)]
    pieces = lax.all_to_all(
        summed, "vocab", split_axis=0, concat_axis=0, tiled=True, axis_index_groups=z_groups
    )
    rel = jnp.sum(pieces.reshape(NZ, NY, 8, depth).astype(F32), axis=0).astype(BF16)
    at = {d: i for i, d in enumerate(order)}
    lookup = jnp.array([at[d] for d in range(NY)], jnp.int32)
    grad_hidden = jnp.concatenate(
        [take(rel, lookup[(i - y) % NY]) for i in range(NY)]
    )

    grad_weight = lax.dot_general(
        hiddens, grads, (((0,), (0,)), ((), ())), preferred_element_type=F32
    ).astype(BF16)

    loss = jnp.sum(kl_row)
    loss = loss + to_core(loss)
    loss = loss + to_y(loss, 2)
    loss = loss + to_y(loss, 1)
    return (loss / tokens, grad_hidden, grad_weight)


def solution(mesh):
    in_specs = (P(None, "hid"), P("hid", "vocab"), P(("vocab", "hid"), None))
    out_specs = (P(), P("vocab", "hid"), P("hid", "vocab"))
    return jax.shard_map(shards, mesh=mesh, in_specs=in_specs, out_specs=out_specs, check_vma=False)
```

time: 649 us -> 189 us (0.29)
  waiting for transfers between devices: 308 us -> 58.3 us
  blocking collectives: 247 us -> 19.3 us
  starting transfers between devices: 0.12 us -> 37.3 us
  other arithmetic: 34.3 us -> 15.6 us
    reduce_scatter x1 -> x0, waiting for transfers between devices: 195 us -> none  [shards(): lax.psum_scatter(lax.dot_general(grad_logits, head_weight, (((1,), (1,)),...]
    psum x2 -> x0, blocking collectives: 142 us -> none  [the longest x1 71.8 us: row_terms(): lax.psum(jnp.sum(probs * (student_log - teacher_log), axis=1), 'vocab')]
    psum x1 -> x0, waiting for transfers between devices: 79.9 us -> none  [shards(): logits = lax.psum(partial_value, 'hid')]
    pmax x1 -> x0, blocking collectives: 76.1 us -> none  [row_terms(): lax.pmax((jnp.max(logits, axis=1), jnp.max(teacher, axis=1)), 'vocab')]
    ppermute x0 -> x24, waiting for transfers between devices: none -> 45.5 us  [the longest x14 40.3 us: to_y(): lax.ppermute(a, 'hid', [(i, (i + 2 * d) % (2 * NY)) for i in range(2 * NY)])]
    all_gather x1 -> x0, waiting for transfers between devices: 33.1 us -> none  [shards(): lax.all_gather(teacher_tiles.reshape(n_vocab, 1, per_dev, vocab_width), '...]
    ppermute x0 -> x24, starting transfers between devices: none -> 22.5 us  [the longest x14 17.7 us: to_y(): lax.ppermute(a, 'hid', [(i, (i + 2 * d) % (2 * NY)) for i in range(2 * NY)])]
    convert_element_type x2 -> x1, other arithmetic: 15.8 us -> 0.5 us  [shards(): (probs * (student_log - teacher_log - kl_row[:, None]) / tokens).astype(B...]
  transfers between devices with their start and end apart: 3 -> 26, of which waited for: 3 -> 15; matrix products, arithmetic and copies ran while one was open for 3% -> 15% of each run, Pallas kernels for 0% -> 0%
where the time goes in v1:
time: 189 us; the launch traced here: 187 us
  waiting for transfers between devices  58.3 us (31%)
  starting transfers between devices  37.3 us (20%)
  matrix products  24 us (13%)
  local copies, waits for them, and re-layouts  19.5 us (10%)
  blocking collectives  19.3 us (10%)
  other arithmetic  15.6 us (8%)
  between operations  12.7 us (7%)
    ppermute x14, waiting for transfers between devices, to_y(): lax.ppermute(a, 'hid', [(i, (i + 2 * d) % (2 * NY)) for i in range(2 * NY)])  40.3 us
    all_to_all x1, blocking collectives, shards(): lax.all_to_all(terms, 'vocab', split_axis=0, concat_axis=0, tiled=True)  19.3 us
    ppermute x14, starting transfers between devices, to_y(): lax.ppermute(a, 'hid', [(i, (i + 2 * d) % (2 * NY)) for i in range(2 * NY)])  17.7 us
    unnamed x28, local copies, waits for them, and re-layouts  13.8 us
    all_to_all x1, starting transfers between devices, shards(): lax.all_to_all(teacher_logits, 'vocab', split_axis=1, concat_axis=0, tile...  11.3 us
    dot_general x3, matrix products, dot(): return jnp.dot(a, head_weight, preferred_element_type=F32)  9.79 us
    dot_general x1, matrix products, shards(): lax.dot_general(hiddens, grads, (((0,), (0,)), ((), ())), preferred_eleme...  9.41 us
    all_to_all x1, waiting for transfers between devices, shards(): lax.all_to_all(summed, 'vocab', split_axis=0, concat_axis=0, tiled=True,...  7.83 us
  transfers between devices with their start and end apart: 26, of which 15 were waited for; matrix products, arithmetic and copies ran while one was open for 15% of the time, Pallas kernels for 0%

profile of v1, /device:TPU:24, one launch (start us, length us, event | category | flops | bytes accessed | tf_op | source)
XLA Modules:
  0.0 186.7 jit_solution(1734500034942453128)
XLA Ops:
  0.8 1.9 %constant_dynamic-update-slice_fusion.16 = (bf16[1024,1024]{1,0:T(8,128)(2,1)}, bf16[128,1024]{1,0:T(8,128)(2,1)S(1)}) fusion(bf16[2,16,4,8,1024]{4,3,2,1,0:T(8,128)(2,1)} %bitcast.92, s32[]{:T(128)S(6)} %select_n.195, s32[]{:T(128)S(6)} %select_n.199), kind=kLoop, calls=%fused_computation.76 | loop fusion | bytes 786440
  2.6 1.7 constant_dynamic-update-slice_fusion.15
  4.4 1.7 constant_dynamic-update-slice_fusion.14
  6.1 1.8 constant_dynamic-update-slice_fusion.13
  11.2 1.7 constant_dynamic-update-slice_fusion.11
  13.0 1.7 constant_dynamic-update-slice_fusion.10
  14.7 3.5 %fusion.12 = f32[384,2048]{1,0:T(8,128)} fusion(bf16[1024,2048]{1,0:T(8,128)(2,1)S(1)} %copy-done, bf16[128,1024]{1,0:T(8,128)(2,1)S(1)} %get-tuple-element.9, bf16[128,1024]{1,0:T(8,128)(2,1)S(1)} %get-tuple-element.11, bf16[128,1024]{1,0:T(8,128)(2,1)S(1)} %get-tuple-element.13), kind=kOutput, calls=%fused_computation.24 | convolution fusion | flops 1612972032 | bytes 8126464 | tf_op jit(solution)/shard_map/dot_general | solution.py:46
  20.4 11.3 %all-to-all-start = ((bf16[4,32,2048]{2,0,1:T(4,128)(2,1)}), bf16[4,32,2048]{2,0,1:T(4,128)(2,1)S(1)}, u32[]{:S(2)}, u32[]{:S(2)}) async-start(bf16[4,32,2048]{2,0,1:T(4,128)(2,1)} %bitcast.11), calls=%async_computation | async-start | bytes 1048576 | tf_op jit(solution)/shard_map/all_to_all | solution.py:60
  31.8 4.6 %fusion.1 = f32[512,2048]{1,0:T(8,128)S(1)} fusion(bf16[1024,2048]{1,0:T(8,128)(2,1)} %param.5, bf16[128,1024]{1,0:T(8,128)(2,1)} %get-tuple-element.15, bf16[128,1024]{1,0:T(8,128)(2,1)S(1)} %get-tuple-element.17, bf16[128,1024]{1,0:T(8,128)(2,1)S(1)} %get-tuple-element.19, bf16[128,1024]{1,0:T(8,128)(2,1)S(1)} %get-tuple-element.21), kind=kOutput, calls=%fused_computation.7 | convolution fusion | flops 2151677952 | bytes 9437184 | tf_op jit(solution)/shard_map/dot_general | solution.py:46
  37.5 3.1 %slice_add_fusion.2 = (f32[128,2048]{1,0:T(8,128)S(1)}, f32[128,2048]{1,0:T(8,128)S(1)}, f32[128,2048]{1,0:T(8,128)S(1)}) fusion(f32[384,2048]{1,0:T(8,128)} %collective-permute-done, f32[512,2048]{1,0:T(8,128)S(1)} %fusion.1, f32[128,2048]{1,0:T(8,128)} %copy-done.3), kind=kLoop, calls=%fused_computation.4 | loop fusion | flops 786432 | bytes 9437184 | tf_op jit(solution)/shard_map/add | solution.py:56
  41.9 1.8 collective-permute-start.6
  43.7 4.9 %all-to-all-done = bf16[4,32,2048]{2,0,1:T(4,128)(2,1)S(1)} async-done(((bf16[4,32,2048]{2,0,1:T(4,128)(2,1)}), bf16[4,32,2048]{2,0,1:T(4,128)(2,1)S(1)}, u32[]{:S(2)}, u32[]{:S(2)}) %all-to-all-start) | async-done | bytes 524320 | tf_op jit(solution)/shard_map/all_to_all | solution.py:60
  49.0 6.5 %collective-permute-done.3 = f32[64,2048]{1,0:T(8,128)S(1)} collective-permute-done((f32[64,2048]{1,0:T(8,128)}, f32[64,2048]{1,0:T(8,128)S(1)}, u32[]{:S(2)}, u32[]{:S(2)}) %collective-permute-start.3) | collective-permute-done | bytes 524320 | tf_op jit(solution)/shard_map/ppermute | solution.py:16
  57.8 2.1 %fusion.35 = (f32[64,2048]{1,0:T(8,128)}, f32[64,2048]{1,0:T(8,128)}) fusion(f32[128,2048]{1,0:T(8,128)S(1)} %get-tuple-element.26, f32[64,2048]{1,0:T(8,128)} %collective-permute-done.6), kind=kLoop, calls=%fused_computation.100 | loop fusion | flops 131072 | bytes 2621440 | tf_op jit(solution)/shard_map/slice | solution.py:59
  61.3 2.5 %collective-permute-start.4 = (f32[64,2048]{1,0:T(8,128)S(1)}, f32[64,2048]{1,0:T(8,128)}, u32[]{:S(2)}, u32[]{:S(2)}) collective-permute-start(f32[64,2048]{1,0:T(8,128)S(1)} %get-tuple-element.33), channel_id=1, source_target_pairs={{0,2},{1,3},{2,4},{3,5},{4,6},{5,7},{6,0},{7,1},{8,10},{9,11},{10,... | collective-permute-start | bytes 1572872 | tf_op jit(solution)/shard_map/ppermute | solution.py:16
  66.1 5.4 %collective-permute-done.5 = f32[64,2048]{1,0:T(8,128)} collective-permute-done((f32[64,2048]{1,0:T(8,128)}, f32[64,2048]{1,0:T(8,128)}, u32[]{:S(2)}, u32[]{:S(2)}) %collective-permute-start.5) | collective-permute-done | bytes 524320 | tf_op jit(solution)/shard_map/ppermute | solution.py:16
  71.5 4.8 %collective-permute-done.7 = f32[64,2048]{1,0:T(8,128)} collective-permute-done((f32[64,2048]{1,0:T(8,128)}, f32[64,2048]{1,0:T(8,128)}, u32[]{:S(2)}, u32[]{:S(2)}) %collective-permute-start.7) | collective-permute-done | bytes 524320 | tf_op jit(solution)/shard_map/ppermute | solution.py:16
  77.6 7.6 %collective-permute-done.1 = f32[64,2048]{1,0:T(8,128)} collective-permute-done((f32[64,2048]{1,0:T(8,128)}, f32[64,2048]{1,0:T(8,128)}, u32[]{:S(2)}, u32[]{:S(2)}) %collective-permute-start.1) | collective-permute-done | bytes 524320 | tf_op jit(solution)/shard_map/ppermute | solution.py:16
  86.5 1.8 fusion.32
  88.7 19.3 %all_to_all.30 = f32[32,8,128]{2,1,0:T(8,128)S(1)} all-to-all(f32[32,8,128]{2,1,0:T(8,128)S(1)} %broadcast_in_dim.2), channel_id=1, replica_groups=mesh['vocab'=32,'hid'=8] {'vocab'}, dimensions={0} | all-to-all | bytes 262144 | tf_op jit(solution)/shard_map/all_to_all | solution.py:80
  109.4 2.0 %collective-permute-start.14 = (bf16[64,2048]{1,0:T(8,128)(2,1)S(1)}, bf16[64,2048]{1,0:T(8,128)(2,1)S(1)}, u32[]{:S(2)}, u32[]{:S(2)}) collective-permute-start(bf16[64,2048]{1,0:T(8,128)(2,1)S(1)} %get-tuple-element.39), channel_id=1, source_target_pairs={{0,6},{1,7},{2,0},{3,1},{4,2},{5,3},{6,4},{7,5},{8,14},{9,15},{10,... | collective-permute-start | bytes 786440 | tf_op jit(solution)/shard_map/ppermute | solution.py:16
  111.5 3.2 %collective-permute-start.17 = (bf16[64,2048]{1,0:T(8,128)(2,1)S(1)}, bf16[64,2048]{1,0:T(8,128)(2,1)S(1)}, u32[]{:S(2)}, u32[]{:S(2)}) collective-permute-start(bf16[64,2048]{1,0:T(8,128)(2,1)S(1)} %get-tuple-element.39), channel_id=1, source_target_pairs={{0,2},{1,3},{2,4},{3,5},{4,6},{5,7},{6,0},{7,1},{8,10},{9,11},{10,... | collective-permute-start | bytes 786440 | tf_op jit(solution)/shard_map/ppermute | solution.py:16
  114.7 4.0 %collective-permute-done.12 = bf16[64,2048]{1,0:T(8,128)(2,1)S(1)} collective-permute-done((bf16[64,2048]{1,0:T(8,128)(2,1)S(1)}, bf16[64,2048]{1,0:T(8,128)(2,1)S(1)}, u32[]{:S(2)}, u32[]{:S(2)}) %collective-permute-start.12) | collective-permute-done | bytes 262176 | tf_op jit(solution)/shard_map/ppermute | solution.py:16
  120.7 2.6 %collective-permute-done.16 = bf16[64,2048]{1,0:T(8,128)(2,1)S(1)} collective-permute-done((bf16[64,2048]{1,0:T(8,128)(2,1)S(1)}, bf16[64,2048]{1,0:T(8,128)(2,1)S(1)}, u32[]{:S(2)}, u32[]{:S(2)}) %collective-permute-start.16) | collective-permute-done | bytes 262176 | tf_op jit(solution)/shard_map/ppermute | solution.py:16
  125.0 2.3 %collective-permute-done.15 = bf16[64,2048]{1,0:T(8,128)(2,1)S(1)} collective-permute-done((bf16[64,2048]{1,0:T(8,128)(2,1)S(1)}, bf16[64,2048]{1,0:T(8,128)(2,1)S(1)}, u32[]{:S(2)}, u32[]{:S(2)}) %collective-permute-start.15) | collective-permute-done | bytes 262176 | tf_op jit(solution)/shard_map/ppermute | solution.py:16
  130.0 4.7 %convolution_convert_fusion.1 = bf16[1024,1024]{1,0:T(8,128)(2,1)S(1)} fusion(bf16[1024,2048]{1,0:T(8,128)(2,1)S(1)} %constant_dynamic-update-slice_fusion, bf16[1024,2048]{1,0:T(8,128)(2,1)S(1)} %copy-done.1), kind=kOutput, calls=%fused_computation.1 | convolution fusion | flops 4296015872 | bytes 10485760 | tf_op jit(solution)/shard_map/dot_general | solution.py:108
  152.0 3.7 %collective-permute-done.10 = f32[]{:T(128)} collective-permute-done((f32[]{:T(128)}, f32[]{:T(128)}, u32[]{:S(2)}, u32[]{:S(2)}) %collective-permute-start.10) | collective-permute-done | bytes 36 | tf_op jit(solution)/shard_map/ppermute | solution.py:16
  158.0 1.9 %collective-permute-done.11 = f32[]{:T(128)} collective-permute-done((f32[]{:T(128)}, f32[]{:T(128)}, u32[]{:S(2)}, u32[]{:S(2)}) %collective-permute-start.11) | collective-permute-done | bytes 36 | tf_op jit(solution)/shard_map/ppermute | solution.py:16
  160.6 2.3 %collective-permute-done.22 = bf16[4,8,8,1024]{3,2,0,1:T(8,128)(2,1)S(1)} collective-permute-done((bf16[4,8,8,1024]{3,2,0,1:T(8,128)(2,1)S(1)}, bf16[4,8,8,1024]{3,2,0,1:T(8,128)(2,1)S(1)}, u32[]{:S(2)}, u32[]{:S(2)}) %collective-permute-start.22) | collective-permute-done | bytes 524320 | tf_op jit(solution)/shard_map/ppermute | solution.py:20
  164.1 3.5 %all-to-all-start.2 = ((bf16[8,32,1024]{2,1,0:T(8,128)(2,1)}), bf16[8,32,1024]{2,1,0:T(8,128)(2,1)S(1)}, u32[]{:S(2)}, u32[]{:S(2)}) async-start(bf16[8,32,1024]{2,1,0:T(8,128)(2,1)} %fusion.18), calls=%async_computation.2 | async-start | bytes 1048576 | tf_op jit(solution)/shard_map/all_to_all | solution.py:127
  167.6 9.4 %convolution_convert_fusion = bf16[1024,2048]{1,0:T(8,128)(2,1)} fusion(bf16[1024,1024]{1,0:T(8,128)(2,1)} %get-tuple-element.8, bf16[1024,2048]{1,0:T(8,128)(2,1)} %copy-done.4), kind=kOutput, calls=%fused_computation | convolution fusion | flops 4297064448 | bytes 10485760 | tf_op jit(solution)/shard_map/dot_general | solution.py:137
  177.0 7.8 %all-to-all-done.2 = bf16[8,32,1024]{2,1,0:T(8,128)(2,1)S(1)} async-done(((bf16[8,32,1024]{2,1,0:T(8,128)(2,1)}), bf16[8,32,1024]{2,1,0:T(8,128)(2,1)S(1)}, u32[]{:S(2)}, u32[]{:S(2)}) %all-to-all-start.2) | async-done | bytes 524320 | tf_op jit(solution)/shard_map/all_to_all | solution.py:127
  (93 shorter events, 36.7 us)
Async XLA Ops:
  0.8 13.9 %copy-start = (bf16[1024,2048]{1,0:T(8,128)(2,1)S(1)}, bf16[1024,2048]{1,0:T(8,128)(2,1)}, u32[]{:S(2)}) copy-start(bf16[1024,2048]{1,0:T(8,128)(2,1)} %param.5) | copy-start | bytes 12582916
  18.2 19.4 %collective-permute-start = (f32[384,2048]{1,0:T(8,128)}, f32[384,2048]{1,0:T(8,128)}, u32[]{:S(2)}, u32[]{:S(2)}) collective-permute-start(f32[384,2048]{1,0:T(8,128)} %fusion.12), channel_id=1, source_target_pairs={{0,1},{1,0},{2,3},{3,2},{4,5},{5,4},{6,7},{7,6},{8,9},{9,8},{10,11... | collective-permute-start | bytes 9437192 | tf_op jit(solution)/shard_map/ppermute | solution.py:12
  19.9 16.6 %collective-permute-start.2 = (f32[128,2048]{1,0:T(8,128)S(1)}, f32[128,2048]{1,0:T(8,128)S(1)}, u32[]{:S(2)}, u32[]{:S(2)}) collective-permute-start(f32[128,2048]{1,0:T(8,128)S(1)} %fusion.23), channel_id=1, source_target_pairs={{0,1},{1,0},{2,3},{3,2},{4,5},{5,4},{6,7},{7,6},{8,9},{9,8},{10,11... | collective-permute-start | bytes 3145736 | tf_op jit(solution)/shard_map/ppermute | solution.py:12
  20.4 28.2 %all-to-all-start = ((bf16[4,32,2048]{2,0,1:T(4,128)(2,1)}), bf16[4,32,2048]{2,0,1:T(4,128)(2,1)S(1)}, u32[]{:S(2)}, u32[]{:S(2)}) async-start(bf16[4,32,2048]{2,0,1:T(4,128)(2,1)} %bitcast.11), calls=%async_computation | async-start | bytes 1048576 | tf_op jit(solution)/shard_map/all_to_all | solution.py:60
  36.4 4.2 %copy-start.2 = (f32[512,2048]{1,0:T(8,128)}, f32[512,2048]{1,0:T(8,128)S(1)}, u32[]{:S(2)}) copy-start(f32[512,2048]{1,0:T(8,128)S(1)} %fusion.1) | copy-start | bytes 12582916
  36.4 1.1 copy-start.3
  41.7 13.8 %collective-permute-start.3 = (f32[64,2048]{1,0:T(8,128)}, f32[64,2048]{1,0:T(8,128)S(1)}, u32[]{:S(2)}, u32[]{:S(2)}) collective-permute-start(f32[64,2048]{1,0:T(8,128)} %get-tuple-element.35), channel_id=1, source_target_pairs={{0,2},{1,3},{2,4},{3,5},{4,6},{5,7},{6,0},{7,1},{8,10},{9,11},{10,... | collective-permute-start | bytes 1572872 | tf_op jit(solution)/shard_map/ppermute | solution.py:16
  41.9 15.9 %collective-permute-start.6 = (f32[64,2048]{1,0:T(8,128)}, f32[64,2048]{1,0:T(8,128)}, u32[]{:S(2)}, u32[]{:S(2)}) collective-permute-start(f32[64,2048]{1,0:T(8,128)} %get-tuple-element.36), channel_id=1, source_target_pairs={{0,6},{1,7},{2,0},{3,1},{4,2},{5,3},{6,4},{7,5},{8,14},{9,15},{10,... | collective-permute-start | bytes 1572872 | tf_op jit(solution)/shard_map/ppermute | solution.py:16
  48.9 14.9 %collective-permute-start.8 = (bf16[16,4,2048]{2,1,0:T(4,128)(2,1)S(1)}, bf16[16,4,2048]{2,1,0:T(4,128)(2,1)S(1)}, u32[]{:S(2)}, u32[]{:S(2)}) collective-permute-start(bf16[16,4,2048]{2,1,0:T(4,128)(2,1)S(1)} %get-tuple-element.45), channel_id=1, source_target_pairs={{0,1},{1,0},{2,3},{3,2},{4,5},{5,4},{6,7},{7,6},{8,9},{9,8},{10,11... | collective-permute-start | bytes 786440 | tf_op jit(solution)/shard_map/ppermute | solution.py:12
  56.3 15.2 %collective-permute-start.5 = (f32[64,2048]{1,0:T(8,128)}, f32[64,2048]{1,0:T(8,128)}, u32[]{:S(2)}, u32[]{:S(2)}) collective-permute-start(f32[64,2048]{1,0:T(8,128)} %get-tuple-element.34), channel_id=1, source_target_pairs={{0,2},{1,3},{2,4},{3,5},{4,6},{5,7},{6,0},{7,1},{8,10},{9,11},{10,... | collective-permute-start | bytes 1572872 | tf_op jit(solution)/shard_map/ppermute | solution.py:16
  60.0 16.4 %collective-permute-start.7 = (f32[64,2048]{1,0:T(8,128)}, f32[64,2048]{1,0:T(8,128)}, u32[]{:S(2)}, u32[]{:S(2)}) collective-permute-start(f32[64,2048]{1,0:T(8,128)} %get-tuple-element.38), channel_id=1, source_target_pairs={{0,6},{1,7},{2,0},{3,1},{4,2},{5,3},{6,4},{7,5},{8,14},{9,15},{10,... | collective-permute-start | bytes 1572872 | tf_op jit(solution)/shard_map/ppermute | solution.py:16
  60.5 24.7 %collective-permute-start.1 = (f32[64,2048]{1,0:T(8,128)}, f32[64,2048]{1,0:T(8,128)}, u32[]{:S(2)}, u32[]{:S(2)}) collective-permute-start(f32[64,2048]{1,0:T(8,128)} %get-tuple-element.37), channel_id=1, source_target_pairs={{0,6},{1,7},{2,0},{3,1},{4,2},{5,3},{6,4},{7,5},{8,14},{9,15},{10,... | collective-permute-start | bytes 1572872 | tf_op jit(solution)/shard_map/ppermute | solution.py:16
  61.3 24.0 %collective-permute-start.4 = (f32[64,2048]{1,0:T(8,128)S(1)}, f32[64,2048]{1,0:T(8,128)}, u32[]{:S(2)}, u32[]{:S(2)}) collective-permute-start(f32[64,2048]{1,0:T(8,128)S(1)} %get-tuple-element.33), channel_id=1, source_target_pairs={{0,2},{1,3},{2,4},{3,5},{4,6},{5,7},{6,0},{7,1},{8,10},{9,11},{10,... | collective-permute-start | bytes 1572872 | tf_op jit(solution)/shard_map/ppermute | solution.py:16
  109.3 9.3 %collective-permute-start.12 = (bf16[64,2048]{1,0:T(8,128)(2,1)S(1)}, bf16[64,2048]{1,0:T(8,128)(2,1)S(1)}, u32[]{:S(2)}, u32[]{:S(2)}) collective-permute-start(bf16[64,2048]{1,0:T(8,128)(2,1)S(1)} %get-tuple-element.40), channel_id=1, source_target_pairs={{0,2},{1,3},{2,4},{3,5},{4,6},{5,7},{6,0},{7,1},{8,10},{9,11},{10,... | collective-permute-start | bytes 786440 | tf_op jit(solution)/shard_map/ppermute | solution.py:16
  109.4 10.3 %collective-permute-start.14 = (bf16[64,2048]{1,0:T(8,128)(2,1)S(1)}, bf16[64,2048]{1,0:T(8,128)(2,1)S(1)}, u32[]{:S(2)}, u32[]{:S(2)}) collective-permute-start(bf16[64,2048]{1,0:T(8,128)(2,1)S(1)} %get-tuple-element.39), channel_id=1, source_target_pairs={{0,6},{1,7},{2,0},{3,1},{4,2},{5,3},{6,4},{7,5},{8,14},{9,15},{10,... | collective-permute-start | bytes 786440 | tf_op jit(solution)/shard_map/ppermute | solution.py:16
  111.4 11.9 %collective-permute-start.16 = (bf16[64,2048]{1,0:T(8,128)(2,1)S(1)}, bf16[64,2048]{1,0:T(8,128)(2,1)S(1)}, u32[]{:S(2)}, u32[]{:S(2)}) collective-permute-start(bf16[64,2048]{1,0:T(8,128)(2,1)S(1)} %get-tuple-element.40), channel_id=1, source_target_pairs={{0,6},{1,7},{2,0},{3,1},{4,2},{5,3},{6,4},{7,5},{8,14},{9,15},{10,... | collective-permute-start | bytes 786440 | tf_op jit(solution)/shard_map/ppermute | solution.py:16
  111.5 11.9 %collective-permute-start.17 = (bf16[64,2048]{1,0:T(8,128)(2,1)S(1)}, bf16[64,2048]{1,0:T(8,128)(2,1)S(1)}, u32[]{:S(2)}, u32[]{:S(2)}) collective-permute-start(bf16[64,2048]{1,0:T(8,128)(2,1)S(1)} %get-tuple-element.39), channel_id=1, source_target_pairs={{0,2},{1,3},{2,4},{3,5},{4,6},{5,7},{6,0},{7,1},{8,10},{9,11},{10,... | collective-permute-start | bytes 786440 | tf_op jit(solution)/shard_map/ppermute | solution.py:16
  118.6 6.4 %collective-permute-start.13 = (bf16[64,2048]{1,0:T(8,128)(2,1)S(1)}, bf16[64,2048]{1,0:T(8,128)(2,1)S(1)}, u32[]{:S(2)}, u32[]{:S(2)}) collective-permute-start(bf16[64,2048]{1,0:T(8,128)(2,1)S(1)} %collective-permute-done.12), channel_id=1, source_target_pairs={{0,2},{1,3},{2,4},{3,5},{4,6},{5,7},{6,0},{7,1},{8,10},{9,11},{10,... | collective-permute-start | bytes 786440 | tf_op jit(solution)/shard_map/ppermute | solution.py:16
  119.7 7.6 %collective-permute-start.15 = (bf16[64,2048]{1,0:T(8,128)(2,1)S(1)}, bf16[64,2048]{1,0:T(8,128)(2,1)S(1)}, u32[]{:S(2)}, u32[]{:S(2)}) collective-permute-start(bf16[64,2048]{1,0:T(8,128)(2,1)S(1)} %collective-permute-done.14), channel_id=1, source_target_pairs={{0,6},{1,7},{2,0},{3,1},{4,2},{5,3},{6,4},{7,5},{8,14},{9,15},{10,... | collective-permute-start | bytes 786440 | tf_op jit(solution)/shard_map/ppermute | solution.py:16
  120.7 9.0 %collective-permute-start.20 = (bf16[128,2048]{1,0:T(8,128)(2,1)S(1)}, bf16[128,2048]{1,0:T(8,128)(2,1)S(1)}, u32[]{:S(2)}, u32[]{:S(2)}) collective-permute-start(bf16[128,2048]{1,0:T(8,128)(2,1)S(1)} %multiply_convert_fusion), channel_id=1, source_target_pairs={{0,1},{1,0},{2,3},{3,2},{4,5},{5,4},{6,7},{7,6},{8,9},{9,8},{10,11... | collective-permute-start | bytes 1572872 | tf_op jit(solution)/shard_map/ppermute | solution.py:12
  123.4 6.2 %collective-permute-start.19 = (bf16[256,2048]{1,0:T(8,128)(2,1)S(1)}, bf16[256,2048]{1,0:T(8,128)(2,1)S(1)}, u32[]{:S(2)}, u32[]{:S(2)}) collective-permute-start(bf16[256,2048]{1,0:T(8,128)(2,1)S(1)} %pad_maximum_fusion), channel_id=1, source_target_pairs={{0,1},{1,0},{2,3},{3,2},{4,5},{5,4},{6,7},{7,6},{8,9},{9,8},{10,11... | collective-permute-start | bytes 3145736 | tf_op jit(solution)/shard_map/ppermute | solution.py:12
  127.4 2.2 %collective-permute-start.18 = (bf16[128,2048]{1,0:T(8,128)(2,1)S(1)}, bf16[128,2048]{1,0:T(8,128)(2,1)S(1)}, u32[]{:S(2)}, u32[]{:S(2)}) collective-permute-start(bf16[128,2048]{1,0:T(8,128)(2,1)S(1)} %pad_maximum_fusion.2), channel_id=1, source_target_pairs={{0,1},{1,0},{2,3},{3,2},{4,5},{5,4},{6,7},{7,6},{8,9},{9,8},{10,11... | collective-permute-start | bytes 1572872 | tf_op jit(solution)/shard_map/ppermute | solution.py:12
  127.8 2.2 %copy-start.1 = (bf16[1024,2048]{1,0:T(8,128)(2,1)S(1)}, bf16[1024,2048]{1,0:T(8,128)(2,1)}, u32[]{:S(2)}) copy-start(bf16[1024,2048]{1,0:T(8,128)(2,1)} %param.5) | copy-start | bytes 12582916
  130.0 4.8 %copy-start.4 = (bf16[1024,2048]{1,0:T(8,128)(2,1)}, bf16[1024,2048]{1,0:T(8,128)(2,1)S(1)}, u32[]{:S(2)}) copy-start(bf16[1024,2048]{1,0:T(8,128)(2,1)S(1)} %constant_dynamic-update-slice_fusion) | copy-start | bytes 12582916
  134.7 4.8 %copy-start.5 = (s32[4]{0:T(128)S(1)}, s32[4]{0:T(128)}, u32[]{:S(2)}) copy-start(s32[4]{0:T(128)} %constant.408.clone) | copy-start | bytes 52
  135.1 25.5 %collective-permute-start.23 = (bf16[4,8,8,1024]{3,2,0,1:T(8,128)(2,1)S(1)}, bf16[4,8,8,1024]{3,2,0,1:T(8,128)(2,1)S(1)}, u32[]{:S(2)}, u32[]{:S(2)}) collective-permute-start(bf16[4,8,8,1024]{3,2,0,1:T(8,128)(2,1)S(1)} %bitcast.103), channel_id=1, source_target_pairs={{0,192},{8,200},{16,208},{24,216},{32,224},{40,232},{48,240},{56,2... | collective-permute-start | bytes 1572872 | tf_op jit(solution)/shard_map/ppermute | solution.py:20
  136.3 26.6 %collective-permute-start.22 = (bf16[4,8,8,1024]{3,2,0,1:T(8,128)(2,1)S(1)}, bf16[4,8,8,1024]{3,2,0,1:T(8,128)(2,1)S(1)}, u32[]{:S(2)}, u32[]{:S(2)}) collective-permute-start(bf16[4,8,8,1024]{3,2,0,1:T(8,128)(2,1)S(1)} %bitcast.104), channel_id=1, source_target_pairs={{0,64},{8,72},{16,80},{24,88},{32,96},{40,104},{48,112},{56,120},{... | collective-permute-start | bytes 1572872 | tf_op jit(solution)/shard_map/ppermute | solution.py:20
  138.1 24.8 %collective-permute-start.21 = (bf16[4,8,8,1024]{3,2,0,1:T(8,128)(2,1)}, bf16[4,8,8,1024]{3,2,0,1:T(8,128)(2,1)S(1)}, u32[]{:S(2)}, u32[]{:S(2)}) collective-permute-start(bf16[4,8,8,1024]{3,2,0,1:T(8,128)(2,1)} %bitcast.91), channel_id=1, source_target_pairs={{0,128},{8,136},{16,144},{24,152},{32,160},{40,168},{48,176},{56,1... | collective-permute-start | bytes 1572872 | tf_op jit(solution)/shard_map/ppermute | solution.py:20
  147.9 1.3 collective-permute-start.9
  150.6 5.1 %collective-permute-start.10 = (f32[]{:T(128)}, f32[]{:T(128)}, u32[]{:S(2)}, u32[]{:S(2)}) collective-permute-start(f32[]{:T(128)} %add.288), channel_id=1, source_target_pairs={{0,4},{1,5},{2,6},{3,7},{4,0},{5,1},{6,2},{7,3},{8,12},{9,13},{10,... | collective-permute-start | bytes 20 | tf_op jit(solution)/shard_map/ppermute | solution.py:16
  156.3 3.6 %collective-permute-start.11 = (f32[]{:T(128)}, f32[]{:T(128)}, u32[]{:S(2)}, u32[]{:S(2)}) collective-permute-start(f32[]{:T(128)} %add.289), channel_id=1, source_target_pairs={{0,2},{1,3},{2,4},{3,5},{4,6},{5,7},{6,0},{7,1},{8,10},{9,11},{10,... | collective-permute-start | bytes 20 | tf_op jit(solution)/shard_map/ppermute | solution.py:16
  164.1 20.7 %all-to-all-start.2 = ((bf16[8,32,1024]{2,1,0:T(8,128)(2,1)}), bf16[8,32,1024]{2,1,0:T(8,128)(2,1)S(1)}, u32[]{:S(2)}, u32[]{:S(2)}) async-start(bf16[8,32,1024]{2,1,0:T(8,128)(2,1)} %fusion.18), calls=%async_computation.2 | async-start | bytes 1048576 | tf_op jit(solution)/shard_map/all_to_all | solution.py:127
